TPU v7x, 32 devices: a whole 2x2x4 slice. The times are simulated.
32 devices in a mesh: ctx: 8 (over y, x, core), head: 4 (over z).
Axes of the slice: x: 2, y: 2, z: 4, core: 2. Of those that a mesh axis runs over, the one named last changes fastest.
Arguments:
- queries: bfloat16 [16384, 8, 128], P('ctx', 'head'), may hold values from -100 to 100
- key_vectors: bfloat16 [16384, 128], P('ctx'), may hold values from -41 to 41
- value_vectors: bfloat16 [16384, 128], P('ctx'), may hold values from -24 to 24
- grad_out: bfloat16 [16384, 8, 128], P('ctx', 'head'), may hold values from -6 to 6
- doc_lengths: int32 [10], replicated, may hold values from 1 to 4096, 16384 in all
Outputs:
- attention_out: bfloat16 [16384, 8, 128], P('ctx', 'head')
- grad_queries: bfloat16 [16384, 8, 128], P('ctx', 'head')
- grad_keys: bfloat16 [16384, 128], P(('ctx', 'head'))
- grad_values: bfloat16 [16384, 128], P(('ctx', 'head'))
Inputs may be any that keep to these rules, and one draw needn't show every extreme that they name: `doc_lengths`: lengths of the packed documents in sequence order; they sum to 16384 and the longest is exactly 4096.
All inputs are finite; a program needn't handle non-finite values.
Results may differ from a plain program's by a relative error of at most 0.012.
Values may be sent and summed in bfloat16 or wider, within the bound.
A program may use at most 192 MiB of HBM per device.

v0:
```python
import jax
import jax.numpy as jnp
from jax import lax
from jax.sharding import PartitionSpec as P

MAXDOC = 4096


masked_value = -1e30


def shifted(x, axis, by):
    length = lax.axis_size(axis)
    pairs = [(i, i + by) for i in range(length) if 0 <= i + by < length]
    return lax.ppermute(x, axis, pairs)


def stretch_number(device_index, half_index, axis_span):
    return jnp.where(half_index == 0, device_index, 2 * axis_span - 1 - device_index)


def doc_number(positions, doc_ends):
    return jnp.sum((doc_ends[None, :] <= positions[:, None]).astype(jnp.int32), axis=1)


def keep_state(carried):
    return carried


def per_device(queries, key_vectors, value_vectors, grad_out, doc_lengths):
    axis_span = lax.axis_size("ctx")
    here_index = lax.axis_index("ctx")
    tok_rows = key_vectors.shape[0]
    stretch_rows = tok_rows // 2
    local_heads = queries.shape[1]
    head_width = key_vectors.shape[1]
    reach_count = (MAXDOC - 1 + stretch_rows - 1) // stretch_rows
    scale_factor = 1.0 / head_width
    doc_ends = jnp.cumsum(doc_lengths)
    packed = jnp.concatenate([key_vectors, value_vectors], axis=1)
    lower_parts = []
    upper_parts = []
    for offset in range(1, reach_count + 1):
        lower_parts.append(shifted(packed, "ctx", offset))
        upper_parts.append(shifted(packed, "ctx", -offset))
    window = jnp.stack(lower_parts[::-1] + [packed] + upper_parts)
    slot_count = 2 * (2 * reach_count + 1)
    key_stretches = window.reshape(slot_count, stretch_rows, 2 * head_width)
    slot_index = jnp.arange(slot_count, dtype=jnp.int32)
    source_device = here_index + slot_index // 2 - reach_count
    source_valid = (source_device >= 0) & (source_device < axis_span)
    slot_stretch = stretch_number(source_device, slot_index % 2, axis_span)
    slot_last_doc = doc_number(slot_stretch * stretch_rows + stretch_rows - 1, doc_ends)
    row_offsets = jnp.arange(stretch_rows, dtype=jnp.int32)
    slot_key_pos = slot_stretch[:, None] * stretch_rows + row_offsets[None, :]
    slot_key_doc = doc_number(slot_key_pos.reshape(-1), doc_ends).reshape(slot_count, stretch_rows)
    row_count = stretch_rows * local_heads

    def slot_logits(slot_number, query_rows, query_pos, query_doc):
        key_block = lax.dynamic_index_in_dim(key_stretches, slot_number, 0, keepdims=False)
        key_part = key_block[:, :head_width]
        value_part = key_block[:, head_width:]
        key_pos = lax.dynamic_index_in_dim(slot_key_pos, slot_number, 0, keepdims=False)
        key_doc = lax.dynamic_index_in_dim(slot_key_doc, slot_number, 0, keepdims=False)
        allowed = (key_doc[None, :] == query_doc[:, None]) & (
            key_pos[None, :] <= query_pos[:, None]
        )
        logits = (
            lax.dot_general(
                query_rows, key_part, (((1,), (1,)), ((), ())), preferred_element_type=jnp.float32
            )
            * scale_factor
        )
        return (logits, allowed, key_part, value_part)

    slot_terms = jnp.zeros((slot_count, stretch_rows, 2 * head_width), jnp.float32)
    out_halves = []
    grad_halves = []
    for half_index in range(2):
        query_stretch = stretch_number(here_index, half_index, axis_span)
        first_row = half_index * stretch_rows
        query_rows = queries[first_row : first_row + stretch_rows].reshape(row_count, head_width)
        dout_rows = grad_out[first_row : first_row + stretch_rows].reshape(row_count, head_width)
        query_pos = (
            query_stretch * stretch_rows + jnp.arange(row_count, dtype=jnp.int32) // local_heads
        )
        query_doc = doc_number(query_pos, doc_ends)
        needed = source_valid & (slot_stretch <= query_stretch) & (slot_last_doc >= query_doc[0])

        def stat_step(slot_number, carried):

            def stat_update(state_in):
                row_max, row_sum = state_in
                logits, allowed, key_part, value_part = slot_logits(
                    slot_number, query_rows, query_pos, query_doc
                )
                new_max = jnp.maximum(
                    row_max, jnp.max(jnp.where(allowed, logits, masked_value), axis=1)
                )
                row_sum = row_sum * jnp.exp(row_max - new_max) + jnp.sum(
                    jnp.where(allowed, jnp.exp(logits - new_max[:, None]), 0.0), axis=1
                )
                return (new_max, row_sum)

            return lax.cond(needed[slot_number], stat_update, keep_state, carried)

        start_stats = (
            jnp.full((row_count,), masked_value, jnp.float32),
            jnp.zeros((row_count,), jnp.float32),
        )
        row_max, row_sum = lax.fori_loop(0, slot_count, stat_step, start_stats)
        log_total = row_max + jnp.log(row_sum)

        def out_step(slot_number, carried):

            def out_update(running):
                logits, allowed, key_part, value_part = slot_logits(
                    slot_number, query_rows, query_pos, query_doc
                )
                probs_low = jnp.where(allowed, jnp.exp(logits - log_total[:, None]), 0.0).astype(
                    jnp.bfloat16
                )
                return running + jnp.dot(probs_low, value_part, preferred_element_type=jnp.float32)

            return lax.cond(needed[slot_number], out_update, keep_state, carried)

        running = lax.fori_loop(
            0, slot_count, out_step, jnp.zeros((row_count, head_width), jnp.float32)
        )
        out_rows = running.astype(jnp.bfloat16)
        delta = jnp.sum(dout_rows.astype(jnp.float32) * out_rows.astype(jnp.float32), axis=1)

        def grad_step(slot_number, carried):

            def grad_update(state_in):
                grad_query, terms_in = state_in
                logits, allowed, key_part, value_part = slot_logits(
                    slot_number, query_rows, query_pos, query_doc
                )
                probs_full = jnp.where(allowed, jnp.exp(logits - log_total[:, None]), 0.0)
                probs_low = probs_full.astype(jnp.bfloat16)
                grad_probs = lax.dot_general(
                    dout_rows,
                    value_part,
                    (((1,), (1,)), ((), ())),
                    preferred_element_type=jnp.float32,
                )
                grad_logits = (probs_full * (grad_probs - delta[:, None])).astype(jnp.bfloat16)
                grad_query = grad_query + jnp.dot(
                    grad_logits, key_part, preferred_element_type=jnp.float32
                )
                key_grad = lax.dot_general(
                    grad_logits,
                    query_rows,
                    (((0,), (0,)), ((), ())),
                    preferred_element_type=jnp.float32,
                )
                value_grad = lax.dot_general(
                    probs_low,
                    dout_rows,
                    (((0,), (0,)), ((), ())),
                    preferred_element_type=jnp.float32,
                )
                previous = lax.dynamic_index_in_dim(terms_in, slot_number, 0, keepdims=False)
                updated = previous + jnp.concatenate([key_grad, value_grad], axis=1)
                terms_in = lax.dynamic_update_index_in_dim(terms_in, updated, slot_number, 0)
                return (grad_query, terms_in)

            return lax.cond(needed[slot_number], grad_update, keep_state, carried)

        grad_query, slot_terms = lax.fori_loop(
            0, slot_count, grad_step, (jnp.zeros((row_count, head_width), jnp.float32), slot_terms)
        )
        out_halves.append(out_rows.reshape(stretch_rows, local_heads, head_width))
        grad_halves.append(
            (grad_query * scale_factor)
            .astype(jnp.bfloat16)
            .reshape(stretch_rows, local_heads, head_width)
        )
    attention_out = jnp.concatenate(out_halves, axis=0)
    grad_queries = jnp.concatenate(grad_halves, axis=0)
    grad_terms = slot_terms.reshape(2 * reach_count + 1, tok_rows, 2 * head_width)
    grad_total = grad_terms[reach_count]
    for offset in range(1, reach_count + 1):
        moved_first = shifted(grad_terms[reach_count - offset][:stretch_rows], "ctx", -offset)
        grad_total = grad_total + jnp.concatenate(
            [moved_first, jnp.zeros_like(moved_first)], axis=0
        )
        grad_total = grad_total + shifted(grad_terms[reach_count + offset], "ctx", offset)
    grad_shares = lax.psum_scatter(grad_total, "head", scatter_dimension=0, tiled=True)
    grad_keys = (grad_shares[:, :head_width] * scale_factor).astype(jnp.bfloat16)
    grad_values = grad_shares[:, head_width:].astype(jnp.bfloat16)
    return (attention_out, grad_queries, grad_keys, grad_values)


def solution(mesh):
    placed = (P("ctx", "head", None), P("ctx", None), P("ctx", None), P("ctx", "head", None), P())
    return jax.shard_map(
        per_device,
        mesh=mesh,
        in_specs=placed,
        out_specs=(
            P("ctx", "head", None),
            P("ctx", "head", None),
            P(("ctx", "head"), None),
            P(("ctx", "head"), None),
        ),
        check_vma=False,
    )
```

profile of v0, /device:TPU:0, one launch (start us, length us, event | category | flops | bytes accessed | tf_op | source)
XLA Modules:
  0.0 815.2 jit_solution(15695034721306874438)
XLA Ops:
  34.7 44.4 %collective-permute-done = bf16[2048,256]{1,0:T(8,128)(2,1)} collective-permute-done((bf16[2048,256]{1,0:T(8,128)(2,1)S(1)}, bf16[2048,256]{1,0:T(8,128)(2,1)}, u32[]{:S(2)}, u32[]{:S(2)}) %collective-permute-start) | collective-permute-done | bytes 1048608 | tf_op jit(solution)/shard_map/ppermute | solution.py:15
  79.2 22.9 %collective-permute-start.3 = (bf16[2048,256]{1,0:T(8,128)(2,1)S(1)}, bf16[2048,256]{1,0:T(8,128)(2,1)S(1)}, u32[]{:S(2)}, u32[]{:S(2)}) collective-permute-start(bf16[2048,256]{1,0:T(8,128)(2,1)S(1)} %constant_dynamic-update-slice_fusion), channel_id=1, source_target_pairs={{0,4},{4,8},{8,12},{12,16},{16,20},{20,24},{24,28},{1,5},{5,9},{9,... | collective-permute-start | bytes 3145736 | tf_op jit(solution)/shard_map/ppermute | solution.py:15
  110.7 19.7 %collective-permute-done.5 = bf16[2048,256]{1,0:T(8,128)(2,1)S(1)} collective-permute-done((bf16[2048,256]{1,0:T(8,128)(2,1)S(1)}, bf16[2048,256]{1,0:T(8,128)(2,1)S(1)}, u32[]{:S(2)}, u32[]{:S(2)}) %collective-permute-start.5) | collective-permute-done | bytes 1048608 | tf_op jit(solution)/shard_map/ppermute | solution.py:15
  135.5 33.6 %while.98 = (s32[]{:T(128)}, f32[2048]{0:T(1024)S(1)}, f32[2048]{0:T(1024)S(1)}, pred[18]{0:T(512)(128)(4,1)S(1)}, s32[18,1024]{1,0:T(8,128)S(1)}, /*index=5*/s3...) while((s32[]{:T(128)}, f32[2048]{0:T(1024)S(1)}, ...), condition=%wide.region_9.10_spmd.clone, body=%wide.region_4.9_spmd.clone.sunk | while | flops 564157440 | bytes 18932064 | solution.py:111
  169.2 31.7 %while.99 = (s32[]{:T(128)}, f32[2048,128]{1,0:T(8,128)S(1)}, pred[18]{0:T(512)(128)(4,1)S(1)}, s32[18,1024]{1,0:T(8,128)S(1)}, s32[2048]{0:T(1024)S(1)}, /*inde...) while((s32[]{:T(128)}, f32[2048,128]{1,0:T(8,128)S(1)}, ...), condition=%wide.region_13.14_spmd.clone, body=%wide.region_10.13_spmd.clone.sunk | while | flops 1088703488 | bytes 4391234 | solution.py:127
  200.9 56.1 %while.100 = (s32[]{:T(128)}, f32[2048]{0:T(1024)S(1)}, f32[2048]{0:T(1024)S(1)}, pred[18]{0:T(512)(128)(4,1)S(1)}, s32[18,1024]{1,0:T(8,128)S(1)}, /*index=5*/s...) while((s32[]{:T(128)}, f32[2048]{0:T(1024)S(1)}, ...), condition=%wide.region_20.21_spmd.clone, body=%wide.region_15.20_spmd.clone.sunk | while | flops 564157440 | bytes 18932064 | solution.py:111
  258.1 56.7 %while.101 = (s32[]{:T(128)}, f32[2048,128]{1,0:T(8,128)}, pred[18]{0:T(512)(128)(4,1)S(1)}, s32[18,1024]{1,0:T(8,128)S(1)}, s32[2048]{0:T(1024)S(1)}, /*index=5...) while((s32[]{:T(128)}, f32[2048,128]{1,0:T(8,128)}, ...), condition=%wide.region_24.25_spmd.clone, body=%wide.region_21.24_spmd.clone.sunk | while | flops 1088703488 | bytes 4391234 | solution.py:127
  283.3 7.6 conditional.21
  316.0 8.9 %broadcast_in_dim.46 = f32[18,1024,256]{1,2,0:T(8,128)} broadcast(f32[]{:T(128)} %constant.302.clone.1), dimensions={} | broadcast | bytes 18874372 | tf_op jit(solution)/shard_map/broadcast_in_dim | solution.py:76
  324.8 42.0 %while.102 = (s32[]{:T(128)}, f32[2048,128]{1,0:T(8,128)S(1)}, f32[18,1024,256]{1,2,0:T(8,128)}, pred[18]{0:T(512)(128)(4,1)S(1)}, s32[18,1024]{1,0:T(8,128)S(1)...) while((s32[]{:T(128)}, f32[2048,128]{1,0:T(8,128)S(1)}, ...), condition=%wide.region_29.30_spmd.clone, body=%wide.region_26.29_spmd.clone.sunk | while | flops 2718714880 | bytes 50307504 | solution.py:171
  337.8 15.9 %conditional.22 = ((f32[2048,128]{1,0:T(8,128)S(1)}, f32[18,1024,256]{1,2,0:T(8,128)})) conditional(s32[]{:T(128)} %bitcast.213, (f32[2048,128]{1,0:T(8,128)S(1)}, f32[18,1024,256]{1,2,0:T(8,128)}) %tuple.288, (s32[]{:T(128)}, s32[18,1024]{1,0:T(8,128)S(1)}, s32[2048]{0:T(1024)S(1)}, s32[18]{0:T(128)S(1)}, s32[]{:T(128)}, ...), branch_computations={%region_27.27_spmd, %region_28.28_spmd.clone} | conditional | flops 2718712832 | bytes 50208884 | solution.py:169
  368.9 86.8 %while.103 = (s32[]{:T(128)}, f32[2048,128]{1,0:T(8,128)S(1)}, f32[18,1024,256]{1,2,0:T(8,128)}, pred[18]{0:T(512)(128)(4,1)S(1)}, s32[18,1024]{1,0:T(8,128)S(1)...) while((s32[]{:T(128)}, f32[2048,128]{1,0:T(8,128)S(1)}, ...), condition=%wide.region_34.35_spmd.clone, body=%wide.region_31.34_spmd.clone.sunk | while | flops 2718714880 | bytes 50307504 | solution.py:171
  382.4 15.7 %conditional.23 = ((f32[2048,128]{1,0:T(8,128)S(1)}, f32[18,1024,256]{1,2,0:T(8,128)})) conditional(s32[]{:T(128)} %bitcast.214, (f32[2048,128]{1,0:T(8,128)S(1)}, f32[18,1024,256]{1,2,0:T(8,128)}) %tuple.291, (s32[]{:T(128)}, s32[18,1024]{1,0:T(8,128)S(1)}, s32[2048]{0:T(1024)S(1)}, s32[18]{0:T(128)S(1)}, s32[]{:T(128)}, ...), branch_computations={%region_32.32_spmd, %region_33.33_spmd.clone} | conditional | flops 2718712832 | bytes 50208884 | solution.py:169
  400.7 15.7 %conditional.23 = ((f32[2048,128]{1,0:T(8,128)S(1)}, f32[18,1024,256]{1,2,0:T(8,128)})) conditional(s32[]{:T(128)} %bitcast.214, (f32[2048,128]{1,0:T(8,128)S(1)}, f32[18,1024,256]{1,2,0:T(8,128)}) %tuple.291, (s32[]{:T(128)}, s32[18,1024]{1,0:T(8,128)S(1)}, s32[2048]{0:T(1024)S(1)}, s32[18]{0:T(128)S(1)}, s32[]{:T(128)}, ...), branch_computations={%region_32.32_spmd, %region_33.33_spmd.clone} | conditional | flops 2718712832 | bytes 50208884 | solution.py:169
  419.1 15.7 %conditional.23 = ((f32[2048,128]{1,0:T(8,128)S(1)}, f32[18,1024,256]{1,2,0:T(8,128)})) conditional(s32[]{:T(128)} %bitcast.214, (f32[2048,128]{1,0:T(8,128)S(1)}, f32[18,1024,256]{1,2,0:T(8,128)}) %tuple.291, (s32[]{:T(128)}, s32[18,1024]{1,0:T(8,128)S(1)}, s32[2048]{0:T(1024)S(1)}, s32[18]{0:T(128)S(1)}, s32[]{:T(128)}, ...), branch_computations={%region_32.32_spmd, %region_33.33_spmd.clone} | conditional | flops 2718712832 | bytes 50208884 | solution.py:169
  437.4 15.7 %conditional.23 = ((f32[2048,128]{1,0:T(8,128)S(1)}, f32[18,1024,256]{1,2,0:T(8,128)})) conditional(s32[]{:T(128)} %bitcast.214, (f32[2048,128]{1,0:T(8,128)S(1)}, f32[18,1024,256]{1,2,0:T(8,128)}) %tuple.291, (s32[]{:T(128)}, s32[18,1024]{1,0:T(8,128)S(1)}, s32[2048]{0:T(1024)S(1)}, s32[18]{0:T(128)S(1)}, s32[]{:T(128)}, ...), branch_computations={%region_32.32_spmd, %region_33.33_spmd.clone} | conditional | flops 2718712832 | bytes 50208884 | solution.py:169
  455.7 18.7 %copy.19 = f32[18,1024,256]{2,1,0:T(8,128)} copy(f32[18,1024,256]{1,2,0:T(8,128)} %get-tuple-element.1357) | data formatting | bytes 37748736 | tf_op jit(solution)/shard_map/while | solution.py:171
  482.6 8.5 %fusion.103 = (f32[2,1024,256]{1,2,0:T(8,128)}, f32[2,1024,256]{1,2,0:T(8,128)}, f32[2,1024,256]{1,2,0:T(8,128)}, f32[2,1024,256]{1,2,0:T(8,128)}, f32[2,1024,256]{1,2,0:T(8,128)}) fusion(f32[18,1024,256]{1,2,0:T(8,128)} %get-tuple-element.1357), kind=kLoop, calls=%fused_computation.193 | loop fusion | bytes 20971520 | tf_op jit(solution)/shard_map/slice | solution.py:183
  502.7 113.8 %collective-permute-start.15 = (f32[2048,256]{1,0:T(8,128)}, f32[2048,256]{1,0:T(8,128)}, u32[]{:S(2)}, u32[]{:S(2)}) collective-permute-start(f32[2048,256]{1,0:T(8,128)} %bitcast.221), channel_id=1, source_target_pairs={{0,16},{4,20},{8,24},{12,28},{1,17},{5,21},{9,25},{13,29},{2,18},{... | collective-permute-start | bytes 6291464 | tf_op jit(solution)/shard_map/ppermute | solution.py:15
  631.6 103.1 %collective-permute-done.10 = f32[1024,256]{1,0:T(8,128)} collective-permute-done((f32[1024,256]{1,0:T(8,128)}, f32[1024,256]{1,0:T(8,128)}, u32[]{:S(2)}, u32[]{:S(2)}) %collective-permute-start.10) | collective-permute-done | bytes 1048608 | tf_op jit(solution)/shard_map/ppermute | solution.py:15
  734.7 12.1 %collective-permute-done.15 = f32[2048,256]{1,0:T(8,128)} collective-permute-done((f32[2048,256]{1,0:T(8,128)}, f32[2048,256]{1,0:T(8,128)}, u32[]{:S(2)}, u32[]{:S(2)}) %collective-permute-start.15) | collective-permute-done | bytes 2097184 | tf_op jit(solution)/shard_map/ppermute | solution.py:15
  754.3 10.1 %pad_maximum_fusion = bf16[2048,2,128]{2,1,0:T(2,128)(2,1)} fusion(bf16[1024,2,128]{2,1,0:T(2,128)(2,1)S(1)} %bitcast.229, bf16[1024,2,128]{2,1,0:T(2,128)(2,1)S(1)} %bitcast.228), kind=kLoop, calls=%fused_computation.145 | loop fusion | flops 524288 | bytes 2097152 | tf_op jit(solution)/shard_map/concatenate | solution.py:180
  764.6 10.1 %pad_maximum_fusion.1 = bf16[2048,2,128]{2,1,0:T(2,128)(2,1)} fusion(bf16[1024,2,128]{2,1,0:T(2,128)(2,1)S(1)} %bitcast.222, bf16[1024,2,128]{2,1,0:T(2,128)(2,1)S(1)} %bitcast.223), kind=kLoop, calls=%fused_computation.146 | loop fusion | flops 524288 | bytes 2097152 | tf_op jit(solution)/shard_map/concatenate | solution.py:181
  774.7 30.0 %reduce-scatter.2.cloned.1.call-done = f32[512,256]{1,0:T(8,128)} async-done(((f32[2048,256]{1,0:T(8,128)}), f32[512,256]{1,0:T(8,128)}) %reduce-scatter.2.cloned.1.call-update) | async-done | bytes 524304 | tf_op jit(solution)/shard_map/reduce_scatter | solution.py:190
  (859 shorter events, 382.7 us)
Async XLA Ops:
  7.2 797.6 %reduce-scatter.2.cloned.1.call-start = ((), (), s32[]{:S(2)}) async-start(), calls=%async_computation.1 | async-start | bytes 2621440 | tf_op jit(solution)/shard_map/reduce_scatter | solution.py:190
  9.5 122.2 %collective-permute-start.7 = (bf16[2048,256]{1,0:T(8,128)(2,1)S(1)}, bf16[2048,256]{1,0:T(8,128)(2,1)S(1)}, u32[]{:S(2)}, u32[]{:S(2)}) collective-permute-start(bf16[2048,256]{1,0:T(8,128)(2,1)S(1)} %constant_dynamic-update-slice_fusion), channel_id=1, source_target_pairs={{16,0},{20,4},{24,8},{28,12},{17,1},{21,5},{25,9},{29,13},{18,2},{... | collective-permute-start | bytes 3145736 | tf_op jit(solution)/shard_map/ppermute | solution.py:15
  10.8 119.6 %collective-permute-start.6 = (bf16[2048,256]{1,0:T(8,128)(2,1)S(1)}, bf16[2048,256]{1,0:T(8,128)(2,1)}, u32[]{:S(2)}, u32[]{:S(2)}) collective-permute-start(bf16[2048,256]{1,0:T(8,128)(2,1)S(1)} %constant_dynamic-update-slice_fusion), channel_id=1, source_target_pairs={{12,0},{16,4},{20,8},{24,12},{28,16},{13,1},{17,5},{21,9},{25,13},... | collective-permute-start | bytes 3145736 | tf_op jit(solution)/shard_map/ppermute | solution.py:15
  12.1 93.9 %collective-permute-start.2 = (bf16[2048,256]{1,0:T(8,128)(2,1)S(1)}, bf16[2048,256]{1,0:T(8,128)(2,1)}, u32[]{:S(2)}, u32[]{:S(2)}) collective-permute-start(bf16[2048,256]{1,0:T(8,128)(2,1)S(1)} %constant_dynamic-update-slice_fusion), channel_id=1, source_target_pairs={{0,8},{4,12},{8,16},{12,20},{16,24},{20,28},{1,9},{5,13},{9,17},{1... | collective-permute-start | bytes 3145736 | tf_op jit(solution)/shard_map/ppermute | solution.py:15
  17.9 85.5 %collective-permute-start.1 = (bf16[2048,256]{1,0:T(8,128)(2,1)S(1)}, bf16[2048,256]{1,0:T(8,128)(2,1)}, u32[]{:S(2)}, u32[]{:S(2)}) collective-permute-start(bf16[2048,256]{1,0:T(8,128)(2,1)S(1)} %constant_dynamic-update-slice_fusion), channel_id=1, source_target_pairs={{0,12},{4,16},{8,20},{12,24},{16,28},{1,13},{5,17},{9,21},{13,25},... | collective-permute-start | bytes 3145736 | tf_op jit(solution)/shard_map/ppermute | solution.py:15
  23.8 55.4 %collective-permute-start = (bf16[2048,256]{1,0:T(8,128)(2,1)S(1)}, bf16[2048,256]{1,0:T(8,128)(2,1)}, u32[]{:S(2)}, u32[]{:S(2)}) collective-permute-start(bf16[2048,256]{1,0:T(8,128)(2,1)S(1)} %constant_dynamic-update-slice_fusion), channel_id=1, source_target_pairs={{0,16},{4,20},{8,24},{12,28},{1,17},{5,21},{9,25},{13,29},{2,18},{... | collective-permute-start | bytes 3145736 | tf_op jit(solution)/shard_map/ppermute | solution.py:15
  79.2 29.9 %collective-permute-start.3 = (bf16[2048,256]{1,0:T(8,128)(2,1)S(1)}, bf16[2048,256]{1,0:T(8,128)(2,1)S(1)}, u32[]{:S(2)}, u32[]{:S(2)}) collective-permute-start(bf16[2048,256]{1,0:T(8,128)(2,1)S(1)} %constant_dynamic-update-slice_fusion), channel_id=1, source_target_pairs={{0,4},{4,8},{8,12},{12,16},{16,20},{20,24},{24,28},{1,5},{5,9},{9,... | collective-permute-start | bytes 3145736 | tf_op jit(solution)/shard_map/ppermute | solution.py:15
  103.4 26.9 %collective-permute-start.5 = (bf16[2048,256]{1,0:T(8,128)(2,1)S(1)}, bf16[2048,256]{1,0:T(8,128)(2,1)S(1)}, u32[]{:S(2)}, u32[]{:S(2)}) collective-permute-start(bf16[2048,256]{1,0:T(8,128)(2,1)S(1)} %constant_dynamic-update-slice_fusion), channel_id=1, source_target_pairs={{8,0},{12,4},{16,8},{20,12},{24,16},{28,20},{9,1},{13,5},{17,9},{2... | collective-permute-start | bytes 3145736 | tf_op jit(solution)/shard_map/ppermute | solution.py:15
  106.0 4.6 collective-permute-start.4
  131.8 3.7 copy-start
  258.1 56.7 %copy-start.3 = (bf16[1024,2,128]{2,1,0:T(2,128)(2,1)S(1)}, bf16[1024,2,128]{2,1,0:T(2,128)(2,1)}, u32[]{:S(2)}) copy-start(bf16[1024,2,128]{2,1,0:T(2,128)(2,1)} %get-tuple-element.2023) | copy-start | bytes 1572868
  324.8 42.0 %copy-start.1 = (f32[2048,128]{1,0:T(8,128)S(1)}, f32[2048,128]{1,0:T(8,128)}, u32[]{:S(2)}) copy-start(f32[2048,128]{1,0:T(8,128)} %get-tuple-element.1353) | copy-start | bytes 3145732
  337.9 3.8 copy-start.4
  400.8 3.6 copy-start.2
  478.7 140.4 %collective-permute-start.8 = (f32[1024,256]{1,0:T(8,128)}, f32[1024,256]{1,0:T(8,128)}, u32[]{:S(2)}, u32[]{:S(2)}) collective-permute-start(f32[1024,256]{1,0:T(8,128)} %get-tuple-element.2012), channel_id=1, source_target_pairs={{4,0},{8,4},{12,8},{16,12},{20,16},{24,20},{28,24},{5,1},{9,5},{13... | collective-permute-start | bytes 3145736 | tf_op jit(solution)/shard_map/ppermute | solution.py:15
  480.0 144.1 %collective-permute-start.14 = (f32[1024,256]{1,0:T(8,128)}, f32[1024,256]{1,0:T(8,128)}, u32[]{:S(2)}, u32[]{:S(2)}) collective-permute-start(f32[1024,256]{1,0:T(8,128)} %get-tuple-element.2013), channel_id=1, source_target_pairs={{16,0},{20,4},{24,8},{28,12},{17,1},{21,5},{25,9},{29,13},{18,2},{... | collective-permute-start | bytes 3145736 | tf_op jit(solution)/shard_map/ppermute | solution.py:15
  481.3 145.9 %collective-permute-start.12 = (f32[1024,256]{1,0:T(8,128)}, f32[1024,256]{1,0:T(8,128)}, u32[]{:S(2)}, u32[]{:S(2)}) collective-permute-start(f32[1024,256]{1,0:T(8,128)} %get-tuple-element.2014), channel_id=1, source_target_pairs={{12,0},{16,4},{20,8},{24,12},{28,16},{13,1},{17,5},{21,9},{25,13},... | collective-permute-start | bytes 3145736 | tf_op jit(solution)/shard_map/ppermute | solution.py:15
  502.7 244.1 %collective-permute-start.15 = (f32[2048,256]{1,0:T(8,128)}, f32[2048,256]{1,0:T(8,128)}, u32[]{:S(2)}, u32[]{:S(2)}) collective-permute-start(f32[2048,256]{1,0:T(8,128)} %bitcast.221), channel_id=1, source_target_pairs={{0,16},{4,20},{8,24},{12,28},{1,17},{5,21},{9,25},{13,29},{2,18},{... | collective-permute-start | bytes 6291464 | tf_op jit(solution)/shard_map/ppermute | solution.py:15
  616.4 130.4 %collective-permute-start.9 = (f32[2048,256]{1,0:T(8,128)}, f32[2048,256]{1,0:T(8,128)}, u32[]{:S(2)}, u32[]{:S(2)}) collective-permute-start(f32[2048,256]{1,0:T(8,128)} %bitcast.220), channel_id=1, source_target_pairs={{0,4},{4,8},{8,12},{12,16},{16,20},{20,24},{24,28},{1,5},{5,9},{9,... | collective-permute-start | bytes 6291464 | tf_op jit(solution)/shard_map/ppermute | solution.py:15
  619.1 127.7 %collective-permute-start.13 = (f32[2048,256]{1,0:T(8,128)}, f32[2048,256]{1,0:T(8,128)}, u32[]{:S(2)}, u32[]{:S(2)}) collective-permute-start(f32[2048,256]{1,0:T(8,128)} %bitcast.219), channel_id=1, source_target_pairs={{0,12},{4,16},{8,20},{12,24},{16,28},{1,13},{5,17},{9,21},{13,25},... | collective-permute-start | bytes 6291464 | tf_op jit(solution)/shard_map/ppermute | solution.py:15
  624.1 122.7 %collective-permute-start.11 = (f32[2048,256]{1,0:T(8,128)}, f32[2048,256]{1,0:T(8,128)}, u32[]{:S(2)}, u32[]{:S(2)}) collective-permute-start(f32[2048,256]{1,0:T(8,128)} %bitcast.218), channel_id=1, source_target_pairs={{0,8},{4,12},{8,16},{12,20},{16,24},{20,28},{1,9},{5,13},{9,17},{1... | collective-permute-start | bytes 6291464 | tf_op jit(solution)/shard_map/ppermute | solution.py:15
  627.2 107.6 %collective-permute-start.10 = (f32[1024,256]{1,0:T(8,128)}, f32[1024,256]{1,0:T(8,128)}, u32[]{:S(2)}, u32[]{:S(2)}) collective-permute-start(f32[1024,256]{1,0:T(8,128)} %get-tuple-element.2015), channel_id=1, source_target_pairs={{8,0},{12,4},{16,8},{20,12},{24,16},{28,20},{9,1},{13,5},{17,9},{2... | collective-permute-start | bytes 3145736 | tf_op jit(solution)/shard_map/ppermute | solution.py:15
  631.6 122.8 %copy-start.5 = (bf16[2048,128]{1,0:T(8,128)(2,1)S(1)}, bf16[2048,128]{1,0:T(8,128)(2,1)}, u32[]{:S(2)}) copy-start(bf16[2048,128]{1,0:T(8,128)(2,1)} %get-tuple-element.1995) | copy-start | bytes 1572868
  631.6 122.8 %copy-start.6 = (bf16[2048,128]{1,0:T(8,128)(2,1)S(1)}, bf16[2048,128]{1,0:T(8,128)(2,1)}, u32[]{:S(2)}) copy-start(bf16[2048,128]{1,0:T(8,128)(2,1)} %get-tuple-element.1993) | copy-start | bytes 1572868
  (3 other events, 10.9 us)
Sparse Core Ops, SparseCore 0:
  754.4 50.2 reduce-scatter.1
where the time goes:
time: 817 us; the launch traced here: 815 us
  waiting for transfers between devices  211 us (26%)
  local copies, waits for them, and re-layouts  174 us (21%)
  starting transfers between devices  172 us (21%)
  matrix products  88 us (11%)
  loops' own time  82.8 us (10%)
  other arithmetic  72.8 us (9%)
  between operations  14.8 us (2%)
    ppermute x16, waiting for transfers between devices, shifted(): return lax.ppermute(x, axis, pairs)  181 us
    ppermute x16, starting transfers between devices, shifted(): return lax.ppermute(x, axis, pairs)  172 us
    reduce_scatter x1, waiting for transfers between devices, per_device(): lax.psum_scatter(grad_total, 'head', scatter_dimension=0, tiled=True)  30 us
    another operation x2, loops' own time, per_device(): lax.fori_loop(0, slot_count, out_step, jnp.zeros((row_count, head_width),...  27 us
    another operation x2, loops' own time, per_device(): row_max, row_sum = lax.fori_loop(0, slot_count, stat_step, start_stats)  26.9 us
    another operation x2, loops' own time, per_device(): lax.fori_loop(0, slot_count, grad_step, (jnp.zeros((row_count, head_width...  26.2 us
    dynamic_slice x36, local copies, waits for them, and re-layouts, stat_step(): return lax.cond(needed[slot_number], stat_update, keep_state, carried)  24.1 us
    dynamic_slice x36, local copies, waits for them, and re-layouts, out_step(): return lax.cond(needed[slot_number], out_update, keep_state, carried)  24.1 us
  transfers between devices with their start and end apart: 17, of which 6 were waited for; matrix products, arithmetic and copies ran while one was open for 7% of the time, Pallas kernels for 0%

commit v1 on v0

v1 whole, which is shorter than its diff:
```python
import functools
import math

import jax
import jax.numpy as jnp
from jax import lax
from jax.experimental import pallas as pl
from jax.experimental.pallas import tpu as pltpu
from jax.sharding import PartitionSpec as P

MAXDOC = 4096
MASKED = -1e30
LOG2E = math.log2(math.e)
TQ = 256
TK = 512


def attention_kernel(
    sizes, first_ref, last_ref, slot_ref, q_ref, do_ref, start_ref, kv_ref, out_ref, dq_ref, dkv_ref, acc_ref
):
    heads, width, rows, tiles, reach, scale = sizes
    step = pl.program_id(0)
    half = step // tiles
    query_stretch = slot_ref[2 * (reach + 1) + half]
    query_first = query_stretch * rows + (step % tiles) * TQ
    lanes = heads * TQ

    @pl.when(step == 0)
    def _():
        def clear(slot, carried):
            acc_ref[slot] = jnp.zeros((rows, 2 * width), jnp.float32)
            return carried

        lax.fori_loop(0, 2 * (reach + 1), clear, 0)

    def heads_first(ref):
        parts = [ref[:, h * width : (h + 1) * width] for h in range(heads)]
        return jnp.concatenate(parts, axis=0) if heads > 1 else parts[0]

    q = heads_first(q_ref)
    do = heads_first(do_ref)
    q_t = q.T
    do_t = do.T
    starts = start_ref[0]
    spread = lax.broadcasted_iota(jnp.int32, (1, lanes), 1) % TQ + query_first - starts
    key_row = lax.broadcasted_iota(jnp.int32, (TK, 1), 0)

    def place(tile):
        stretch = tile * TK // rows
        slot = slot_ref[half * (reach + 1) + query_stretch - stretch]
        return slot, pl.multiple_of(tile * TK - stretch * rows, TK)

    def logits2(tile, key_part):
        s = jnp.dot(key_part, q_t, preferred_element_type=jnp.float32) * (scale * LOG2E)
        behind = (key_row + tile * TK) - starts
        return jnp.where((behind >= 0) & (behind <= spread), s, MASKED)

    def forward(tile, carried):
        top, total, acc = carried
        slot, row = place(tile)
        key_part = kv_ref[slot, pl.ds(row, TK), :width]
        value_part = kv_ref[slot, pl.ds(row, TK), width:]
        s = logits2(tile, key_part)
        new_top = jnp.maximum(top, jnp.max(s, axis=0, keepdims=True))
        p = jnp.exp2(s - new_top)
        shrink = jnp.exp2(top - new_top)
        total = total * shrink + jnp.sum(p, axis=0, keepdims=True)
        acc = acc * shrink + lax.dot_general(
            value_part, p.astype(jnp.bfloat16), (((0,), (0,)), ((), ())), preferred_element_type=jnp.float32
        )
        return new_top, total, acc

    tile_low = first_ref[step] // TK
    tile_high = (query_first + TQ - 1) // TK + 1
    top, total, acc = lax.fori_loop(
        tile_low,
        tile_high,
        forward,
        (
            jnp.full((1, lanes), MASKED, jnp.float32),
            jnp.zeros((1, lanes), jnp.float32),
            jnp.zeros((width, lanes), jnp.float32),
        ),
    )
    out_t = (acc / total).astype(jnp.bfloat16)
    log_total = top + jnp.log2(total)
    delta = jnp.sum(do_t.astype(jnp.float32) * out_t.astype(jnp.float32), axis=0, keepdims=True)
    out = out_t.T
    for h in range(heads):
        out_ref[:, h * width : (h + 1) * width] = out[h * TQ : (h + 1) * TQ]

    def backward(tile, dq_t):
        slot, row = place(tile)
        key_part = kv_ref[slot, pl.ds(row, TK), :width]
        value_part = kv_ref[slot, pl.ds(row, TK), width:]
        p = jnp.exp2(logits2(tile, key_part) - log_total)
        dp = jnp.dot(value_part, do_t, preferred_element_type=jnp.float32)
        ds = (p * (dp - delta)).astype(jnp.bfloat16)
        acc_ref[slot, pl.ds(row, TK), :width] += jnp.dot(ds, q, preferred_element_type=jnp.float32)
        acc_ref[slot, pl.ds(row, TK), width:] += jnp.dot(
            p.astype(jnp.bfloat16), do, preferred_element_type=jnp.float32
        )
        return dq_t + lax.dot_general(
            key_part, ds, (((0,), (0,)), ((), ())), preferred_element_type=jnp.float32
        )

    dq_t = lax.fori_loop(tile_low, tile_high, backward, jnp.zeros((width, lanes), jnp.float32))
    dq = (dq_t * scale).astype(jnp.bfloat16).T
    for h in range(heads):
        dq_ref[:, h * width : (h + 1) * width] = dq[h * TQ : (h + 1) * TQ]

    @pl.when(step == 2 * tiles - 1)
    def _():
        def finish(slot, carried):
            dkv_ref[slot] = acc_ref[slot].astype(jnp.bfloat16)
            return carried

        lax.fori_loop(0, 2 * (reach + 1), finish, 0)


def run_attention(queries, grad_out, window, first, last, slots, starts, rows, reach):
    tok_rows, heads, width = queries.shape
    tiles = rows // TQ
    sizes = (heads, width, rows, tiles, reach, 1.0 / width)
    slot_count = window.shape[0]
    row_spec = pl.BlockSpec((TQ, heads * width), lambda t, *_: (t, 0))
    all_spec = pl.BlockSpec((slot_count, rows, 2 * width), lambda t, *_: (0, 0, 0))
    out, dq, dkv = pl.pallas_call(
        functools.partial(attention_kernel, sizes),
        out_shape=(
            jax.ShapeDtypeStruct((tok_rows, heads * width), jnp.bfloat16),
            jax.ShapeDtypeStruct((tok_rows, heads * width), jnp.bfloat16),
            jax.ShapeDtypeStruct(window.shape, jnp.bfloat16),
        ),
        grid_spec=pltpu.PrefetchScalarGridSpec(
            num_scalar_prefetch=3,
            grid=(2 * tiles,),
            in_specs=[
                row_spec,
                row_spec,
                pl.BlockSpec((1, 1, heads * TQ), lambda t, *_: (t, 0, 0)),
                all_spec,
            ],
            out_specs=(row_spec, row_spec, all_spec),
            scratch_shapes=[pltpu.VMEM((slot_count, rows, 2 * width), jnp.float32)],
        ),
        compiler_params=pltpu.CompilerParams(
            dimension_semantics=("arbitrary",), vmem_limit_bytes=56 * 1024 * 1024
        ),
    )(
        first,
        last,
        slots,
        queries.reshape(tok_rows, heads * width),
        grad_out.reshape(tok_rows, heads * width),
        starts,
        window,
    )
    return out.reshape(queries.shape), dq.reshape(queries.shape), dkv


def extra_pairs(n, k):
    pairs = []
    for below in range(1, k):
        if k < 2 * below + 1 and k >= below + 1 and below < n:
            pairs.append((n - k + below, n - 1 - below))
    return pairs


def per_device(queries, key_vectors, value_vectors, grad_out, doc_lengths):
    n = lax.axis_size("ctx")
    here = lax.axis_index("ctx")
    tok_rows, heads, width = queries.shape
    rows = tok_rows // 2
    reach = (MAXDOC - 1 + rows - 1) // rows
    tiles = rows // TQ
    packed = jnp.concatenate([key_vectors, value_vectors], axis=1)
    low, high = packed[:rows], packed[rows:]

    def move(x, pairs):
        return lax.ppermute(x, "ctx", pairs)

    def up(k):
        return [(i, i + k) for i in range(n - k)]

    def down(k):
        return [(i + k, i) for i in range(n - k)]

    def back(pairs):
        return [(b, a) for a, b in pairs]

    lows = [move(low, up(k)) for k in range(1, reach + 1)]
    highs = []
    for k in range(1, reach + 1):
        part = move(high, down(k))
        pairs = extra_pairs(n, k)
        if pairs:
            part = jnp.where(here >= n - k, move(low, pairs), part)
        highs.append(part)
    window = jnp.stack([low] + lows + [high] + highs)

    steps = jnp.arange(reach + 1, dtype=jnp.int32)
    again = 2 * here - (2 * n - 1) + steps
    slots = jnp.concatenate(
        [
            steps,
            jnp.where((again >= 0) & (again <= reach), again, steps + reach + 1),
            jnp.stack([here, 2 * n - 1 - here]),
        ]
    ).astype(jnp.int32)

    doc_ends = jnp.cumsum(doc_lengths)
    stretch = jnp.stack([here, 2 * n - 1 - here]).astype(jnp.int32)
    pos = (stretch[:, None] * rows + jnp.arange(rows, dtype=jnp.int32)[None, :]).reshape(-1)
    begin = jnp.max(jnp.where(doc_ends[None, :] <= pos[:, None], doc_ends[None, :], 0), axis=1)
    begin = begin.astype(jnp.int32).reshape(2 * tiles, TQ)
    starts = jnp.tile(begin, (1, heads)).reshape(2 * tiles, 1, heads * TQ)
    out, dq, dkv = run_attention(
        queries, grad_out, window, begin[:, 0], begin[:, -1], slots, starts, rows, reach
    )

    low_total = dkv[0].astype(jnp.float32)
    high_total = dkv[reach + 1].astype(jnp.float32)
    for k in range(1, reach + 1):
        low_total = low_total + move(dkv[k], back(up(k))).astype(jnp.float32)
        term = dkv[reach + 1 + k]
        high_total = high_total + move(term, back(down(k))).astype(jnp.float32)
        pairs = extra_pairs(n, k)
        if pairs:
            low_total = low_total + move(term, back(pairs)).astype(jnp.float32)
    total = jnp.concatenate([low_total, high_total], axis=0)
    shares = lax.psum_scatter(total, "head", scatter_dimension=0, tiled=True)
    grad_keys = (shares[:, :width] * (1.0 / width)).astype(jnp.bfloat16)
    grad_values = shares[:, width:].astype(jnp.bfloat16)
    return out, dq, grad_keys, grad_values


def solution(mesh):
    placed = (P("ctx", "head", None), P("ctx", None), P("ctx", None), P("ctx", "head", None), P())
    return jax.shard_map(
        per_device,
        mesh=mesh,
        in_specs=placed,
        out_specs=(
            P("ctx", "head", None),
            P("ctx", "head", None),
            P(("ctx", "head"), None),
            P(("ctx", "head"), None),
        ),
        check_vma=False,
    )
```

time: 817 us -> 283 us (0.35)
  local copies, waits for them, and re-layouts: 174 us -> 21.2 us
  starting transfers between devices: 172 us -> 40.9 us
  matrix products: 88 us -> 0 us
  loops' own time: 82.8 us -> 0 us
  waiting for transfers between devices: 211 us -> 136 us
  other arithmetic: 72.8 us -> 9.6 us
  Pallas kernels: 0 us -> 58.9 us
    ppermute x16 -> x22, starting transfers between devices: 172 us -> 40.9 us  [move(): return lax.ppermute(x, 'ctx', pairs)]
    ppermute x16 -> x22, waiting for transfers between devices: 181 us -> 88.4 us  [move(): return lax.ppermute(x, 'ctx', pairs)]
    dot_general x35 -> x0, matrix products: 88 us -> none  [the longest x5 23.4 us: out_update(): jnp.dot(probs_low, value_part, preferred_element_type=jnp.float32)]
    another operation x114 -> x0, loops' own time: 82.8 us -> none  [the longest x2 27 us: per_device(): lax.fori_loop(0, slot_count, out_step, jnp.zeros((row_count, head_width),...]
    dynamic_slice x123 -> x0, local copies, waits for them, and re-layouts: 80.5 us -> none  [the longest x36 24.1 us: stat_step(): return lax.cond(needed[slot_number], stat_update, keep_state, carried)]
    pallas_call x0 -> x1, Pallas kernels: none -> 58.9 us  [run_attention(): pl.pallas_call(functools.partial(attention_kernel, sizes), out_shape=(jax...]
    slice x12 -> x3, local copies, waits for them, and re-layouts: 35 us -> 3.44 us  [the longest x1 1.62 us: per_device(): grad_values = shares[:, width:].astype(jnp.bfloat16)]
    while x1 -> x0, local copies, waits for them, and re-layouts: 18.7 us -> none  [per_device(): lax.fori_loop(0, slot_count, grad_step, (jnp.zeros((row_count, head_width...]
  transfers between devices with their start and end apart: 17 -> 23, of which waited for: 6 -> 10; matrix products, arithmetic and copies ran while one was open for 7% -> 6% of each run, Pallas kernels for 0% -> 0%
where the time goes in v1:
time: 283 us; the launch traced here: 281 us
  waiting for transfers between devices  136 us (48%)
  Pallas kernels  58.9 us (21%)
  starting transfers between devices  40.9 us (14%)
  local copies, waits for them, and re-layouts  21.2 us (7%)
  between operations  14.3 us (5%)
  other arithmetic  9.6 us (3%)
    ppermute x22, waiting for transfers between devices, move(): return lax.ppermute(x, 'ctx', pairs)  88.4 us
    pallas_call x1, Pallas kernels, run_attention(): pl.pallas_call(functools.partial(attention_kernel, sizes), out_shape=(jax...  58.9 us
    reduce_scatter x1, waiting for transfers between devices, per_device(): shares = lax.psum_scatter(total, 'head', scatter_dimension=0, tiled=True)  48.1 us
    ppermute x22, starting transfers between devices, move(): return lax.ppermute(x, 'ctx', pairs)  40.9 us
    unnamed x15, local copies, waits for them, and re-layouts  8.2 us
  transfers between devices with their start and end apart: 23, of which 10 were waited for; matrix products, arithmetic and copies ran while one was open for 6% of the time, Pallas kernels for 0%

profile of v1, /device:TPU:0, one launch (start us, length us, event | category | flops | bytes accessed | tf_op | source)
XLA Modules:
  0.0 281.4 jit_solution(15718118202316801786)
XLA Ops:
  10.6 3.2 %collective-permute-start = (bf16[1024,256]{1,0:T(8,128)(2,1)}, bf16[1024,256]{1,0:T(8,128)(2,1)}, u32[]{:S(2)}, u32[]{:S(2)}) collective-permute-start(bf16[1024,256]{1,0:T(8,128)(2,1)} %get-tuple-element.23), channel_id=1, source_target_pairs={{0,4},{4,8},{8,12},{12,16},{16,20},{20,24},{24,28},{1,5},{5,9},{9,... | collective-permute-start | bytes 1572872 | tf_op jit(solution)/shard_map/ppermute | solution.py:181
  13.7 3.6 %collective-permute-start.1 = (bf16[1024,256]{1,0:T(8,128)(2,1)}, bf16[1024,256]{1,0:T(8,128)(2,1)S(1)}, u32[]{:S(2)}, u32[]{:S(2)}) collective-permute-start(bf16[1024,256]{1,0:T(8,128)(2,1)} %get-tuple-element.23), channel_id=1, source_target_pairs={{0,8},{4,12},{8,16},{12,20},{16,24},{20,28},{1,9},{5,13},{9,17},{1... | collective-permute-start | bytes 1572872 | tf_op jit(solution)/shard_map/ppermute | solution.py:181
  17.4 4.3 %collective-permute-start.2 = (bf16[1024,256]{1,0:T(8,128)(2,1)}, bf16[1024,256]{1,0:T(8,128)(2,1)S(1)}, u32[]{:S(2)}, u32[]{:S(2)}) collective-permute-start(bf16[1024,256]{1,0:T(8,128)(2,1)} %get-tuple-element.23), channel_id=1, source_target_pairs={{0,12},{4,16},{8,20},{12,24},{16,28},{1,13},{5,17},{9,21},{13,25},... | collective-permute-start | bytes 1572872 | tf_op jit(solution)/shard_map/ppermute | solution.py:181
  24.8 3.2 %copy_bitcast_fusion = (bf16[2048,256]{1,0:T(8,128)(2,1)}, bf16[2048,256]{1,0:T(8,128)(2,1)}) fusion(bf16[256,8,2,128]{3,2,1,0:T(2,128)(2,1)} %bitcast.57, bf16[256,8,2,128]{3,2,1,0:T(2,128)(2,1)} %bitcast.58), kind=kLoop, calls=%fused_computation.1 | loop fusion | bytes 4194304 | tf_op jit(solution)/shard_map/reshape | solution.py:155
  30.9 1.4 collective-permute-start.4
  32.3 1.9 bitcast_dynamic-update-slice_fusion.8
  36.4 2.3 collective-permute-done.2
  40.2 10.7 %collective-permute-done.3 = bf16[1024,256]{1,0:T(8,128)(2,1)S(1)} collective-permute-done((bf16[1024,256]{1,0:T(8,128)(2,1)}, bf16[1024,256]{1,0:T(8,128)(2,1)S(1)}, u32[]{:S(2)}, u32[]{:S(2)}) %collective-permute-start.3) | collective-permute-done | bytes 524320 | tf_op jit(solution)/shard_map/ppermute | solution.py:181
  56.8 2.0 collective-permute-done.6
  59.7 3.3 %collective-permute-done.8 = bf16[1024,256]{1,0:T(8,128)(2,1)S(1)} collective-permute-done((bf16[1024,256]{1,0:T(8,128)(2,1)}, bf16[1024,256]{1,0:T(8,128)(2,1)S(1)}, u32[]{:S(2)}, u32[]{:S(2)}) %collective-permute-start.8) | collective-permute-done | bytes 524320 | tf_op jit(solution)/shard_map/ppermute | solution.py:181
  64.0 14.7 %collective-permute-done.10 = bf16[1024,256]{1,0:T(8,128)(2,1)S(1)} collective-permute-done((bf16[1024,256]{1,0:T(8,128)(2,1)S(1)}, bf16[1024,256]{1,0:T(8,128)(2,1)S(1)}, u32[]{:S(2)}, u32[]{:S(2)}) %collective-permute-start.10) | collective-permute-done | bytes 524320 | tf_op jit(solution)/shard_map/ppermute | solution.py:181
  79.6 58.9 %shard_map.84 = (bf16[2048,256]{1,0:T(8,128)(2,1)}, bf16[2048,256]{1,0:T(8,128)(2,1)}, bf16[10,1024,256]{2,1,0:T(8,128)(2,1)}) custom-call(s32[8]{0:T(128)} %get-tuple-element.11.first_ref, s32[8]{0:T(128)} %get-tuple-element.10.last_ref, s32[12]{0:T(128)} %pad_add_fusion.slot_ref, bf16[2048,256]{1,0:T(8,128)(2,1)} %get-tuple-element.25.q_ref, ...), custom_call_target="tpu_custom_call" | custom-call | tf_op jit(solution)/shard_map/pallas_call | solution.py:128
  138.6 2.4 slice_bitcast_fusion.7
  146.3 14.2 %collective-permute-done.11 = bf16[1024,256]{1,0:T(8,128)(2,1)S(1)} collective-permute-done((bf16[1024,256]{1,0:T(8,128)(2,1)S(1)}, bf16[1024,256]{1,0:T(8,128)(2,1)S(1)}, u32[]{:S(2)}, u32[]{:S(2)}) %collective-permute-start.11) | collective-permute-done | bytes 524320 | tf_op jit(solution)/shard_map/ppermute | solution.py:181
  161.8 21.5 %collective-permute-done.12 = bf16[1024,256]{1,0:T(8,128)(2,1)S(1)} collective-permute-done((bf16[1024,256]{1,0:T(8,128)(2,1)S(1)}, bf16[1024,256]{1,0:T(8,128)(2,1)S(1)}, u32[]{:S(2)}, u32[]{:S(2)}) %collective-permute-start.12) | collective-permute-done | bytes 524320 | tf_op jit(solution)/shard_map/ppermute | solution.py:181
  183.3 1.5 collective-permute-start.19
  186.9 9.8 %collective-permute-start.20 = (bf16[1024,256]{1,0:T(8,128)(2,1)S(1)}, bf16[1024,256]{1,0:T(8,128)(2,1)S(1)}, u32[]{:S(2)}, u32[]{:S(2)}) collective-permute-start(bf16[1024,256]{1,0:T(8,128)(2,1)S(1)} %get-tuple-element.18), channel_id=1, source_target_pairs={{0,12},{4,16},{8,20},{12,24},{16,28},{1,13},{5,17},{9,21},{13,25},... | collective-permute-start | bytes 1572872 | tf_op jit(solution)/shard_map/ppermute | solution.py:181
  198.0 5.3 %collective-permute-done.20 = bf16[1024,256]{1,0:T(8,128)(2,1)S(1)} collective-permute-done((bf16[1024,256]{1,0:T(8,128)(2,1)S(1)}, bf16[1024,256]{1,0:T(8,128)(2,1)S(1)}, u32[]{:S(2)}, u32[]{:S(2)}) %collective-permute-start.20) | collective-permute-done | bytes 524320 | tf_op jit(solution)/shard_map/ppermute | solution.py:181
  203.3 14.2 %collective-permute-done.21 = bf16[1024,256]{1,0:T(8,128)(2,1)S(1)} collective-permute-done((bf16[1024,256]{1,0:T(8,128)(2,1)S(1)}, bf16[1024,256]{1,0:T(8,128)(2,1)S(1)}, u32[]{:S(2)}, u32[]{:S(2)}) %collective-permute-start.21) | collective-permute-done | bytes 524320 | tf_op jit(solution)/shard_map/ppermute | solution.py:181
  217.5 2.0 fusion.8
  219.5 1.5 pad_maximum_fusion
  223.3 48.1 %reduce-scatter.2.cloned.1.call-done = f32[512,256]{1,0:T(8,128)} async-done(((f32[2048,256]{1,0:T(8,128)}), f32[512,256]{1,0:T(8,128)}) %reduce-scatter.2.cloned.1.call-update) | async-done | bytes 524304 | tf_op jit(solution)/shard_map/reduce_scatter | solution.py:232
  271.3 1.6 fusion.9
  273.0 1.6 slice.89
  (63 shorter events, 33.8 us)
Async XLA Ops:
  7.2 264.2 %reduce-scatter.2.cloned.1.call-start = ((), (), s32[]{:S(2)}) async-start(), calls=%async_computation.1 | async-start | bytes 2621440 | tf_op jit(solution)/shard_map/reduce_scatter | solution.py:232
  10.6 20.4 %collective-permute-start = (bf16[1024,256]{1,0:T(8,128)(2,1)}, bf16[1024,256]{1,0:T(8,128)(2,1)}, u32[]{:S(2)}, u32[]{:S(2)}) collective-permute-start(bf16[1024,256]{1,0:T(8,128)(2,1)} %get-tuple-element.23), channel_id=1, source_target_pairs={{0,4},{4,8},{8,12},{12,16},{16,20},{20,24},{24,28},{1,5},{5,9},{9,... | collective-permute-start | bytes 1572872 | tf_op jit(solution)/shard_map/ppermute | solution.py:181
  13.7 20.5 %collective-permute-start.1 = (bf16[1024,256]{1,0:T(8,128)(2,1)}, bf16[1024,256]{1,0:T(8,128)(2,1)S(1)}, u32[]{:S(2)}, u32[]{:S(2)}) collective-permute-start(bf16[1024,256]{1,0:T(8,128)(2,1)} %get-tuple-element.23), channel_id=1, source_target_pairs={{0,8},{4,12},{8,16},{12,20},{16,24},{20,28},{1,9},{5,13},{9,17},{1... | collective-permute-start | bytes 1572872 | tf_op jit(solution)/shard_map/ppermute | solution.py:181
  17.4 21.3 %collective-permute-start.2 = (bf16[1024,256]{1,0:T(8,128)(2,1)}, bf16[1024,256]{1,0:T(8,128)(2,1)S(1)}, u32[]{:S(2)}, u32[]{:S(2)}) collective-permute-start(bf16[1024,256]{1,0:T(8,128)(2,1)} %get-tuple-element.23), channel_id=1, source_target_pairs={{0,12},{4,16},{8,20},{12,24},{16,28},{1,13},{5,17},{9,21},{13,25},... | collective-permute-start | bytes 1572872 | tf_op jit(solution)/shard_map/ppermute | solution.py:181
  21.7 29.2 %collective-permute-start.3 = (bf16[1024,256]{1,0:T(8,128)(2,1)}, bf16[1024,256]{1,0:T(8,128)(2,1)S(1)}, u32[]{:S(2)}, u32[]{:S(2)}) collective-permute-start(bf16[1024,256]{1,0:T(8,128)(2,1)} %get-tuple-element.23), channel_id=1, source_target_pairs={{0,16},{4,20},{8,24},{12,28},{1,17},{5,21},{9,25},{13,29},{2,18},{... | collective-permute-start | bytes 1572872 | tf_op jit(solution)/shard_map/ppermute | solution.py:181
  23.0 32.5 %collective-permute-start.5 = (bf16[1024,256]{1,0:T(8,128)(2,1)}, bf16[1024,256]{1,0:T(8,128)(2,1)S(1)}, u32[]{:S(2)}, u32[]{:S(2)}) collective-permute-start(bf16[1024,256]{1,0:T(8,128)(2,1)} %get-tuple-element.23), channel_id=1, source_target_pairs={{28,24},{29,25},{30,26},{31,27}} | collective-permute-start | bytes 1572872 | tf_op jit(solution)/shard_map/ppermute | solution.py:181
  30.9 24.6 %copy-start.2 = (bf16[1024,256]{1,0:T(8,128)(2,1)S(1)}, bf16[1024,256]{1,0:T(8,128)(2,1)}, u32[]{:S(2)}) copy-start(bf16[1024,256]{1,0:T(8,128)(2,1)} %get-tuple-element.22) | copy-start | bytes 1572868
  30.9 23.0 %collective-permute-start.4 = (bf16[1024,256]{1,0:T(8,128)(2,1)}, bf16[1024,256]{1,0:T(8,128)(2,1)S(1)}, u32[]{:S(2)}, u32[]{:S(2)}) collective-permute-start(bf16[1024,256]{1,0:T(8,128)(2,1)} %get-tuple-element.22), channel_id=1, source_target_pairs={{4,0},{8,4},{12,8},{16,12},{20,16},{24,20},{28,24},{5,1},{9,5},{13... | collective-permute-start | bytes 1572872 | tf_op jit(solution)/shard_map/ppermute | solution.py:181
  34.2 24.5 %collective-permute-start.6 = (bf16[1024,256]{1,0:T(8,128)(2,1)}, bf16[1024,256]{1,0:T(8,128)(2,1)S(1)}, u32[]{:S(2)}, u32[]{:S(2)}) collective-permute-start(bf16[1024,256]{1,0:T(8,128)(2,1)} %get-tuple-element.22), channel_id=1, source_target_pairs={{8,0},{12,4},{16,8},{20,12},{24,16},{28,20},{9,1},{13,5},{17,9},{2... | collective-permute-start | bytes 1572872 | tf_op jit(solution)/shard_map/ppermute | solution.py:181
  38.7 21.0 %collective-permute-start.7 = (bf16[1024,256]{1,0:T(8,128)(2,1)}, bf16[1024,256]{1,0:T(8,128)(2,1)S(1)}, u32[]{:S(2)}, u32[]{:S(2)}) collective-permute-start(bf16[1024,256]{1,0:T(8,128)(2,1)} %get-tuple-element.23), channel_id=1, source_target_pairs={{28,20},{29,21},{30,22},{31,23}} | collective-permute-start | bytes 1572872 | tf_op jit(solution)/shard_map/ppermute | solution.py:181
  50.9 12.1 %collective-permute-start.8 = (bf16[1024,256]{1,0:T(8,128)(2,1)}, bf16[1024,256]{1,0:T(8,128)(2,1)S(1)}, u32[]{:S(2)}, u32[]{:S(2)}) collective-permute-start(bf16[1024,256]{1,0:T(8,128)(2,1)} %get-tuple-element.22), channel_id=1, source_target_pairs={{12,0},{16,4},{20,8},{24,12},{28,16},{13,1},{17,5},{21,9},{25,13},... | collective-permute-start | bytes 1572872 | tf_op jit(solution)/shard_map/ppermute | solution.py:181
  53.9 10.0 %collective-permute-start.9 = (bf16[1024,256]{1,0:T(8,128)(2,1)}, bf16[1024,256]{1,0:T(8,128)(2,1)S(1)}, u32[]{:S(2)}, u32[]{:S(2)}) collective-permute-start(bf16[1024,256]{1,0:T(8,128)(2,1)} %get-tuple-element.23), channel_id=1, source_target_pairs={{24,20},{28,16},{25,21},{29,17},{26,22},{30,18},{27,23},{31,19}} | collective-permute-start | bytes 1572872 | tf_op jit(solution)/shard_map/ppermute | solution.py:181
  55.5 23.2 %collective-permute-start.10 = (bf16[1024,256]{1,0:T(8,128)(2,1)S(1)}, bf16[1024,256]{1,0:T(8,128)(2,1)S(1)}, u32[]{:S(2)}, u32[]{:S(2)}) collective-permute-start(bf16[1024,256]{1,0:T(8,128)(2,1)S(1)} %copy-done.2), channel_id=1, source_target_pairs={{16,0},{20,4},{24,8},{28,12},{17,1},{21,5},{25,9},{29,13},{18,2},{... | collective-permute-start | bytes 1572872 | tf_op jit(solution)/shard_map/ppermute | solution.py:181
  141.0 19.5 %collective-permute-start.11 = (bf16[1024,256]{1,0:T(8,128)(2,1)S(1)}, bf16[1024,256]{1,0:T(8,128)(2,1)S(1)}, u32[]{:S(2)}, u32[]{:S(2)}) collective-permute-start(bf16[1024,256]{1,0:T(8,128)(2,1)S(1)} %get-tuple-element.14), channel_id=1, source_target_pairs={{4,0},{8,4},{12,8},{16,12},{20,16},{24,20},{28,24},{5,1},{9,5},{13... | collective-permute-start | bytes 1572872 | tf_op jit(solution)/shard_map/ppermute | solution.py:181
  142.3 41.0 %collective-permute-start.12 = (bf16[1024,256]{1,0:T(8,128)(2,1)S(1)}, bf16[1024,256]{1,0:T(8,128)(2,1)S(1)}, u32[]{:S(2)}, u32[]{:S(2)}) collective-permute-start(bf16[1024,256]{1,0:T(8,128)(2,1)S(1)} %get-tuple-element.21), channel_id=1, source_target_pairs={{8,0},{12,4},{16,8},{20,12},{24,16},{28,20},{9,1},{13,5},{17,9},{2... | collective-permute-start | bytes 1572872 | tf_op jit(solution)/shard_map/ppermute | solution.py:181
  143.6 41.2 %collective-permute-start.13 = (bf16[1024,256]{1,0:T(8,128)(2,1)S(1)}, bf16[1024,256]{1,0:T(8,128)(2,1)S(1)}, u32[]{:S(2)}, u32[]{:S(2)}) collective-permute-start(bf16[1024,256]{1,0:T(8,128)(2,1)S(1)} %get-tuple-element.20), channel_id=1, source_target_pairs={{24,28},{25,29},{26,30},{27,31}} | collective-permute-start | bytes 1572872 | tf_op jit(solution)/shard_map/ppermute | solution.py:181
  144.3 41.2 %collective-permute-start.14 = (bf16[1024,256]{1,0:T(8,128)(2,1)S(1)}, bf16[1024,256]{1,0:T(8,128)(2,1)S(1)}, u32[]{:S(2)}, u32[]{:S(2)}) collective-permute-start(bf16[1024,256]{1,0:T(8,128)(2,1)S(1)} %get-tuple-element.19), channel_id=1, source_target_pairs={{12,0},{16,4},{20,8},{24,12},{28,16},{13,1},{17,5},{21,9},{25,13},... | collective-permute-start | bytes 1572872 | tf_op jit(solution)/shard_map/ppermute | solution.py:181
  145.6 41.3 %collective-permute-start.15 = (bf16[1024,256]{1,0:T(8,128)(2,1)S(1)}, bf16[1024,256]{1,0:T(8,128)(2,1)S(1)}, u32[]{:S(2)}, u32[]{:S(2)}) collective-permute-start(bf16[1024,256]{1,0:T(8,128)(2,1)S(1)} %get-tuple-element.18), channel_id=1, source_target_pairs={{20,28},{21,29},{22,30},{23,31}} | collective-permute-start | bytes 1572872 | tf_op jit(solution)/shard_map/ppermute | solution.py:181
  160.5 36.1 %collective-permute-start.16 = (bf16[1024,256]{1,0:T(8,128)(2,1)S(1)}, bf16[1024,256]{1,0:T(8,128)(2,1)S(1)}, u32[]{:S(2)}, u32[]{:S(2)}) collective-permute-start(bf16[1024,256]{1,0:T(8,128)(2,1)S(1)} %get-tuple-element.17), channel_id=1, source_target_pairs={{16,0},{20,4},{24,8},{28,12},{17,1},{21,5},{25,9},{29,13},{18,2},{... | collective-permute-start | bytes 1572872 | tf_op jit(solution)/shard_map/ppermute | solution.py:181
  183.3 14.7 %collective-permute-start.19 = (bf16[1024,256]{1,0:T(8,128)(2,1)S(1)}, bf16[1024,256]{1,0:T(8,128)(2,1)S(1)}, u32[]{:S(2)}, u32[]{:S(2)}) collective-permute-start(bf16[1024,256]{1,0:T(8,128)(2,1)S(1)} %get-tuple-element.20), channel_id=1, source_target_pairs={{0,8},{4,12},{8,16},{12,20},{16,24},{20,28},{1,9},{5,13},{9,17},{1... | collective-permute-start | bytes 1572872 | tf_op jit(solution)/shard_map/ppermute | solution.py:181
  184.8 13.2 %collective-permute-start.17 = (bf16[1024,256]{1,0:T(8,128)(2,1)S(1)}, bf16[1024,256]{1,0:T(8,128)(2,1)S(1)}, u32[]{:S(2)}, u32[]{:S(2)}) collective-permute-start(bf16[1024,256]{1,0:T(8,128)(2,1)S(1)} %get-tuple-element.16), channel_id=1, source_target_pairs={{20,24},{16,28},{21,25},{17,29},{22,26},{18,30},{23,27},{19,31}} | collective-permute-start | bytes 1572872 | tf_op jit(solution)/shard_map/ppermute | solution.py:181
  185.5 12.5 %collective-permute-start.18 = (bf16[1024,256]{1,0:T(8,128)(2,1)S(1)}, bf16[1024,256]{1,0:T(8,128)(2,1)S(1)}, u32[]{:S(2)}, u32[]{:S(2)}) collective-permute-start(bf16[1024,256]{1,0:T(8,128)(2,1)S(1)} %get-tuple-element.15), channel_id=1, source_target_pairs={{0,4},{4,8},{8,12},{12,16},{16,20},{20,24},{24,28},{1,5},{5,9},{9,... | collective-permute-start | bytes 1572872 | tf_op jit(solution)/shard_map/ppermute | solution.py:181
  186.9 16.4 %collective-permute-start.20 = (bf16[1024,256]{1,0:T(8,128)(2,1)S(1)}, bf16[1024,256]{1,0:T(8,128)(2,1)S(1)}, u32[]{:S(2)}, u32[]{:S(2)}) collective-permute-start(bf16[1024,256]{1,0:T(8,128)(2,1)S(1)} %get-tuple-element.18), channel_id=1, source_target_pairs={{0,12},{4,16},{8,20},{12,24},{16,28},{1,13},{5,17},{9,21},{13,25},... | collective-permute-start | bytes 1572872 | tf_op jit(solution)/shard_map/ppermute | solution.py:181
  196.6 20.9 %collective-permute-start.21 = (bf16[1024,256]{1,0:T(8,128)(2,1)S(1)}, bf16[1024,256]{1,0:T(8,128)(2,1)S(1)}, u32[]{:S(2)}, u32[]{:S(2)}) collective-permute-start(bf16[1024,256]{1,0:T(8,128)(2,1)S(1)} %get-tuple-element.16), channel_id=1, source_target_pairs={{0,16},{4,20},{8,24},{12,28},{1,17},{5,21},{9,25},{13,29},{2,18},{... | collective-permute-start | bytes 1572872 | tf_op jit(solution)/shard_map/ppermute | solution.py:181
  (2 other events, 4.2 us)
Sparse Core Ops, SparseCore 0:
  221.2 50.1 reduce-scatter.1

commit v2 on v1

--- a/solution.py
+++ b/solution.py
@@ -167,6 +167,139 @@
     return pairs
 
 
+def gather_kernel(n, reach, x_ref, window_ref, send_sem, extra_sem, pass_sem, recv_sem, local_sem):
+    here = lax.axis_index("ctx")
+    core = here % 2
+    sibling = here + 1 - 2 * core
+    rows = window_ref.shape[1]
+    part_rows = rows // 2
+
+    barrier = pltpu.get_barrier_semaphore()
+    for by in range(1, n):
+        pl.semaphore_signal(
+            barrier, inc=1, device_id={"ctx": (here + by) % n}, device_id_type=pl.DeviceIdType.MESH
+        )
+    pl.semaphore_wait(barrier, n - 1)
+
+    def slot_of(f, k):
+        return f * (reach + 1) + k
+
+    def own(f, p):
+        return x_ref.at[pl.ds(f * rows + p * part_rows, part_rows)]
+
+    def into(f, k, p):
+        return window_ref.at[slot_of(f, k), pl.ds(p * part_rows, part_rows)]
+
+    def copy(src, f, k, p, sem, device):
+        return pltpu.make_async_remote_copy(
+            src_ref=src,
+            dst_ref=into(f, k, p),
+            send_sem=sem,
+            recv_sem=recv_sem.at[slot_of(f, k), p],
+            device_id={"ctx": device},
+            device_id_type=pl.DeviceIdType.MESH,
+        )
+
+    locals_ = [
+        pltpu.make_async_copy(
+            x_ref.at[pl.ds(f * rows, rows)], window_ref.at[slot_of(f, 0)], local_sem.at[f]
+        )
+        for f in range(2)
+    ]
+    for c in locals_:
+        c.start()
+
+    def near(f, device_core):
+        return device_core == f
+
+    direct = []
+    for k in range(reach, 0, -1):
+        for f in range(2):
+            target = here + k if f == 0 else here - k
+            valid = target < n if f == 0 else target >= 0
+            target_near = near(f, (core + k) % 2)
+            for p in range(2):
+                sent = jnp.where(
+                    target_near, p == 0 or k == reach, p == 1 or k == 1
+                )
+                direct.append((valid & sent, copy(own(f, p), f, k, p, send_sem.at[slot_of(f, k), p], target)))
+        for source, target in extra_pairs(n, k):
+            for p in range(2):
+                is_near = target % 2 == 1
+                if (is_near and (p == 0 or k == reach)) or (not is_near and (p == 1 or source == target + 1)):
+                    direct.append(
+                        (here == source, copy(own(0, p), 1, k, p, extra_sem.at[k - 1, target % 2, p], target))
+                    )
+    for when, c in direct:
+        pl.when(when)(c.start)
+
+    def has(f, k):
+        if f == 0:
+            return here - k >= 0
+        found = here + k < n
+        for source, target in extra_pairs(n, k):
+            found = found | (here == target)
+        return found
+
+    passed = []
+    arrivals = []
+    for k in range(1, reach + 1):
+        for f in range(2):
+            present = has(f, k)
+            here_near = near(f, core)
+            whole = jnp.where(here_near, k == reach, k == 1)
+            for source, target in extra_pairs(n, k) if f == 1 else []:
+                if source == target + 1 and target % 2 == 0:
+                    whole = whole | (here == target)
+            for p in range(2):
+                from_source = whole | (here_near == (p == 0))
+                next_k = k + 1 if p == 0 else k - 1
+                forwards = 1 <= next_k <= reach
+                if forwards:
+                    c = copy(into(f, k, p), f, next_k, p, pass_sem.at[slot_of(f, k)], sibling)
+                    when = present & (here_near == (p == 0)) & jnp.logical_not(whole)
+                    arrived = copy(into(f, k, p), f, k, p, pass_sem.at[slot_of(f, k)], sibling)
+                    passed.append((when, c, arrived))
+                    arrivals.append((present & jnp.logical_not(when), arrived))
+                else:
+                    arrived = copy(into(f, k, p), f, k, p, pass_sem.at[slot_of(f, k)], sibling)
+                    arrivals.append((present, arrived))
+    for when, c, arrived in passed:
+
+        @pl.when(when)
+        def _():
+            arrived.wait_recv()
+            c.start()
+
+    for when, arrived in arrivals:
+        pl.when(when)(arrived.wait_recv)
+    for when, c in direct:
+        pl.when(when)(c.wait_send)
+    for when, c, arrived in passed:
+        pl.when(when)(c.wait_send)
+    for c in locals_:
+        c.wait()
+
+
+def gather(packed, n, reach):
+    rows, columns = packed.shape[0] // 2, packed.shape[1]
+    slots = 2 * (reach + 1)
+    return pl.pallas_call(
+        functools.partial(gather_kernel, n, reach),
+        out_shape=jax.ShapeDtypeStruct((slots, rows, columns), packed.dtype),
+        in_specs=[pl.BlockSpec(memory_space=pl.ANY)],
+        out_specs=pl.BlockSpec(memory_space=pl.ANY),
+        scratch_shapes=[
+            pltpu.SemaphoreType.DMA((slots, 2)),
+            pltpu.SemaphoreType.DMA((reach, 2, 2)),
+            pltpu.SemaphoreType.DMA((slots,)),
+            pltpu.SemaphoreType.DMA((slots, 2)),
+            pltpu.SemaphoreType.DMA((2,)),
+        ],
+        compiler_params=pltpu.CompilerParams(collective_id=0, has_side_effects=True),
+    )(packed)
+
+
 def per_device(queries, key_vectors, value_vectors, grad_out, doc_lengths):
     n = lax.axis_size("ctx")
     here = lax.axis_index("ctx")
@@ -175,7 +308,6 @@
     reach = (MAXDOC - 1 + rows - 1) // rows
     tiles = rows // TQ
     packed = jnp.concatenate([key_vectors, value_vectors], axis=1)
-    low, high = packed[:rows], packed[rows:]
 
     def move(x, pairs):
         return lax.ppermute(x, "ctx", pairs)
@@ -189,15 +321,7 @@
     def back(pairs):
         return [(b, a) for a, b in pairs]
 
-    lows = [move(low, up(k)) for k in range(1, reach + 1)]
-    highs = []
-    for k in range(1, reach + 1):
-        part = move(high, down(k))
-        pairs = extra_pairs(n, k)
-        if pairs:
-            part = jnp.where(here >= n - k, move(low, pairs), part)
-        highs.append(part)
-    window = jnp.stack([low] + lows + [high] + highs)
+    window = gather(packed, n, reach)
 
     steps = jnp.arange(reach + 1, dtype=jnp.int32)
     again = 2 * here - (2 * n - 1) + steps
@@ -228,9 +352,9 @@
         pairs = extra_pairs(n, k)
         if pairs:
             low_total = low_total + move(term, back(pairs)).astype(jnp.float32)
-    total = jnp.concatenate([low_total, high_total], axis=0)
+    total = jnp.concatenate([low_total, high_total], axis=0).astype(jnp.bfloat16)
     shares = lax.psum_scatter(total, "head", scatter_dimension=0, tiled=True)
-    grad_keys = (shares[:, :width] * (1.0 / width)).astype(jnp.bfloat16)
+    grad_keys = (shares[:, :width].astype(jnp.float32) * (1.0 / width)).astype(jnp.bfloat16)
     grad_values = shares[:, width:].astype(jnp.bfloat16)
     return out, dq, grad_keys, grad_values
 

time: 283 us -> 240 us (0.85); the launches traced: 281 us -> 241 us
  waiting for transfers between devices: 136 us -> 53.4 us
  starting transfers between devices: 40.9 us -> 80 us
  Pallas kernels: 58.9 us -> 75.3 us
  local copies, waits for them, and re-layouts: 21.2 us -> 9.74 us
    ppermute x22 -> x11, waiting for transfers between devices: 88.4 us -> 17.1 us  [move(): return lax.ppermute(x, 'ctx', pairs)]
    ppermute x22 -> x11, starting transfers between devices: 40.9 us -> 80 us  [move(): return lax.ppermute(x, 'ctx', pairs)]
    pallas_call x0 -> x1, Pallas kernels: none -> 37.4 us  [gather(): pl.pallas_call(functools.partial(gather_kernel, n, reach), out_shape=jax....]
    pallas_call x1, Pallas kernels: 58.9 us -> 38 us  [run_attention(): pl.pallas_call(functools.partial(attention_kernel, sizes), out_shape=(jax...]
    reduce_scatter x1, waiting for transfers between devices: 48.1 us -> 36.3 us  [per_device(): shares = lax.psum_scatter(total, 'head', scatter_dimension=0, tiled=True)]
    unnamed x15 -> x9, local copies, waits for them, and re-layouts: 8.2 us -> 0.55 us
  transfers between devices with their start and end apart: 23 -> 12, of which waited for: 10 -> 4; matrix products, arithmetic and copies ran while one was open for 6% -> 1% of each run, Pallas kernels for 0% -> 0%
where the time goes in v2:
time: 240 us; the launch traced here: 241 us
  starting transfers between devices  80 us (33%)
  Pallas kernels  75.3 us (31%)
  waiting for transfers between devices  53.4 us (22%)
  between operations  14.2 us (6%)
  local copies, waits for them, and re-layouts  9.74 us (4%)
  other arithmetic  8.62 us (4%)
    ppermute x11, starting transfers between devices, move(): return lax.ppermute(x, 'ctx', pairs)  80 us
    pallas_call x1, Pallas kernels, run_attention(): pl.pallas_call(functools.partial(attention_kernel, sizes), out_shape=(jax...  38 us
    pallas_call x1, Pallas kernels, gather(): pl.pallas_call(functools.partial(gather_kernel, n, reach), out_shape=jax....  37.4 us
    reduce_scatter x1, waiting for transfers between devices, per_device(): shares = lax.psum_scatter(total, 'head', scatter_dimension=0, tiled=True)  36.3 us
    ppermute x11, waiting for transfers between devices, move(): return lax.ppermute(x, 'ctx', pairs)  17.1 us
  transfers between devices with their start and end apart: 12, of which 4 were waited for; matrix products, arithmetic and copies ran while one was open for 1% of the time, Pallas kernels for 0%

profile of v2, /device:TPU:0, one launch (start us, length us, event | category | flops | bytes accessed | tf_op | source)
XLA Modules:
  0.0 241.3 jit_solution(546411807118974610)
XLA Ops:
  7.4 0.8 reduce-window.8
  9.7 2.3 pad_maximum_fusion.x_ref
  12.0 37.4 %shard_map.84.kv_ref = bf16[10,1024,256]{2,1,0:T(8,128)(2,1)} custom-call(bf16[2048,256]{1,0:T(8,128)(2,1)} %pad_maximum_fusion.x_ref), custom_call_target="tpu_custom_call" | custom-call | tf_op jit(solution)/shard_map/pallas_call | solution.py:287
  50.0 1.6 copy_bitcast_fusion
  51.6 38.0 %shard_map.85 = (bf16[2048,256]{1,0:T(8,128)(2,1)}, bf16[2048,256]{1,0:T(8,128)(2,1)}, bf16[10,1024,256]{2,1,0:T(8,128)(2,1)}) custom-call(s32[8]{0:T(128)} %get-tuple-element.11.first_ref, s32[8]{0:T(128)} %get-tuple-element.10.last_ref, s32[12]{0:T(128)} %pad_add_fusion.slot_ref, bf16[2048,256]{1,0:T(8,128)(2,1)} %get-tuple-element.23.q_ref, ...), custom_call_target="tpu_custom_call" | custom-call | tf_op jit(solution)/shard_map/pallas_call | solution.py:128
  89.6 2.4 %slice_bitcast_fusion.7 = (bf16[1024,256]{1,0:T(8,128)(2,1)S(1)}, bf16[1024,256]{1,0:T(8,128)(2,1)S(1)}, bf16[1024,256]{1,0:T(8,128)(2,1)S(1)}, bf16[1024,256]{1...) fusion(bf16[10,1024,256]{2,1,0:T(8,128)(2,1)} %get-tuple-element.9), kind=kLoop, calls=%fused_computation.24 | loop fusion | bytes 8388608 | tf_op jit(solution)/shard_map/squeeze | solution.py:349
  92.0 1.3 collective-permute-start
  93.3 34.3 %collective-permute-start.7 = (bf16[1024,256]{1,0:T(8,128)(2,1)S(1)}, bf16[1024,256]{1,0:T(8,128)(2,1)S(1)}, u32[]{:S(2)}, u32[]{:S(2)}) collective-permute-start(bf16[1024,256]{1,0:T(8,128)(2,1)S(1)} %get-tuple-element.15), channel_id=1, source_target_pairs={{0,4},{4,8},{8,12},{12,16},{16,20},{20,24},{24,28},{1,5},{5,9},{9,... | collective-permute-start | bytes 1572872 | tf_op jit(solution)/shard_map/ppermute | solution.py:313
  127.5 1.3 collective-permute-start.5
  128.8 1.3 collective-permute-start.3
  130.1 1.3 collective-permute-start.1
  131.4 6.5 %collective-permute-start.10 = (bf16[1024,256]{1,0:T(8,128)(2,1)S(1)}, bf16[1024,256]{1,0:T(8,128)(2,1)S(1)}, u32[]{:S(2)}, u32[]{:S(2)}) collective-permute-start(bf16[1024,256]{1,0:T(8,128)(2,1)S(1)} %get-tuple-element.16), channel_id=1, source_target_pairs={{0,16},{4,20},{8,24},{12,28},{1,17},{5,21},{9,25},{13,29},{2,18},{... | collective-permute-start | bytes 1572872 | tf_op jit(solution)/shard_map/ppermute | solution.py:313
  138.7 4.8 %collective-permute-done.5 = bf16[1024,256]{1,0:T(8,128)(2,1)S(1)} collective-permute-done((bf16[1024,256]{1,0:T(8,128)(2,1)S(1)}, bf16[1024,256]{1,0:T(8,128)(2,1)S(1)}, u32[]{:S(2)}, u32[]{:S(2)}) %collective-permute-start.5) | collective-permute-done | bytes 524320 | tf_op jit(solution)/shard_map/ppermute | solution.py:313
  143.5 29.0 %collective-permute-start.9 = (bf16[1024,256]{1,0:T(8,128)(2,1)S(1)}, bf16[1024,256]{1,0:T(8,128)(2,1)S(1)}, u32[]{:S(2)}, u32[]{:S(2)}) collective-permute-start(bf16[1024,256]{1,0:T(8,128)(2,1)S(1)} %get-tuple-element.18), channel_id=1, source_target_pairs={{0,12},{4,16},{8,20},{12,24},{16,28},{1,13},{5,17},{9,21},{13,25},... | collective-permute-start | bytes 1572872 | tf_op jit(solution)/shard_map/ppermute | solution.py:313
  173.3 3.0 %collective-permute-start.8 = (bf16[1024,256]{1,0:T(8,128)(2,1)S(1)}, bf16[1024,256]{1,0:T(8,128)(2,1)S(1)}, u32[]{:S(2)}, u32[]{:S(2)}) collective-permute-start(bf16[1024,256]{1,0:T(8,128)(2,1)S(1)} %get-tuple-element.20), channel_id=1, source_target_pairs={{0,8},{4,12},{8,16},{12,20},{16,24},{20,28},{1,9},{5,13},{9,17},{1... | collective-permute-start | bytes 1572872 | tf_op jit(solution)/shard_map/ppermute | solution.py:313
  177.0 2.2 collective-permute-done.9
  179.2 10.0 %collective-permute-done.8 = bf16[1024,256]{1,0:T(8,128)(2,1)S(1)} collective-permute-done((bf16[1024,256]{1,0:T(8,128)(2,1)S(1)}, bf16[1024,256]{1,0:T(8,128)(2,1)S(1)}, u32[]{:S(2)}, u32[]{:S(2)}) %collective-permute-start.8) | collective-permute-done | bytes 524320 | tf_op jit(solution)/shard_map/ppermute | solution.py:313
  189.2 2.0 fusion.10
  191.2 1.0 pad_maximum_fusion.1
  192.8 1.1 reshape.94
  193.9 1.1 reshape.95
  195.0 36.3 %reduce-scatter.2.cloned.1.call-done = bf16[512,256]{1,0:T(8,128)(2,1)} async-done(((bf16[2048,256]{1,0:T(8,128)(2,1)}), bf16[512,256]{1,0:T(8,128)(2,1)}) %reduce-scatter.2.cloned.1.call-update) | async-done | bytes 262160 | tf_op jit(solution)/shard_map/reduce_scatter | solution.py:356
  231.3 1.6 slice.59
  232.9 1.6 multiply_convert_fusion
  (32 shorter events, 4.9 us)
Async XLA Ops:
  7.2 224.1 %reduce-scatter.2.cloned.1.call-start = ((), (), s32[]{:S(2)}) async-start(), calls=%async_computation.1 | async-start | bytes 1310720 | tf_op jit(solution)/shard_map/reduce_scatter | solution.py:356
  12.0 38.0 %copy-start.2 = (bf16[2048,2,128]{2,1,0:T(2,128)(2,1)S(1)}, bf16[2048,2,128]{2,1,0:T(2,128)(2,1)}, u32[]{:S(2)}) copy-start(bf16[2048,2,128]{2,1,0:T(2,128)(2,1)} %param.8) | copy-start | bytes 3145732
  12.0 38.0 %copy-start.3 = (bf16[2048,2,128]{2,1,0:T(2,128)(2,1)S(1)}, bf16[2048,2,128]{2,1,0:T(2,128)(2,1)}, u32[]{:S(2)}) copy-start(bf16[2048,2,128]{2,1,0:T(2,128)(2,1)} %param.5) | copy-start | bytes 3145732
  92.0 39.5 %collective-permute-start = (bf16[1024,256]{1,0:T(8,128)(2,1)S(1)}, bf16[1024,256]{1,0:T(8,128)(2,1)S(1)}, u32[]{:S(2)}, u32[]{:S(2)}) collective-permute-start(bf16[1024,256]{1,0:T(8,128)(2,1)S(1)} %get-tuple-element.14), channel_id=1, source_target_pairs={{4,0},{8,4},{12,8},{16,12},{20,16},{24,20},{28,24},{5,1},{9,5},{13... | collective-permute-start | bytes 1572872 | tf_op jit(solution)/shard_map/ppermute | solution.py:313
  93.3 44.7 %collective-permute-start.7 = (bf16[1024,256]{1,0:T(8,128)(2,1)S(1)}, bf16[1024,256]{1,0:T(8,128)(2,1)S(1)}, u32[]{:S(2)}, u32[]{:S(2)}) collective-permute-start(bf16[1024,256]{1,0:T(8,128)(2,1)S(1)} %get-tuple-element.15), channel_id=1, source_target_pairs={{0,4},{4,8},{8,12},{12,16},{16,20},{20,24},{24,28},{1,5},{5,9},{9,... | collective-permute-start | bytes 1572872 | tf_op jit(solution)/shard_map/ppermute | solution.py:313
  127.5 16.0 %collective-permute-start.5 = (bf16[1024,256]{1,0:T(8,128)(2,1)S(1)}, bf16[1024,256]{1,0:T(8,128)(2,1)S(1)}, u32[]{:S(2)}, u32[]{:S(2)}) collective-permute-start(bf16[1024,256]{1,0:T(8,128)(2,1)S(1)} %get-tuple-element.17), channel_id=1, source_target_pairs={{16,0},{20,4},{24,8},{28,12},{17,1},{21,5},{25,9},{29,13},{18,2},{... | collective-permute-start | bytes 1572872 | tf_op jit(solution)/shard_map/ppermute | solution.py:313
  128.8 43.7 %collective-permute-start.3 = (bf16[1024,256]{1,0:T(8,128)(2,1)S(1)}, bf16[1024,256]{1,0:T(8,128)(2,1)S(1)}, u32[]{:S(2)}, u32[]{:S(2)}) collective-permute-start(bf16[1024,256]{1,0:T(8,128)(2,1)S(1)} %get-tuple-element.19), channel_id=1, source_target_pairs={{12,0},{16,4},{20,8},{24,12},{28,16},{13,1},{17,5},{21,9},{25,13},... | collective-permute-start | bytes 1572872 | tf_op jit(solution)/shard_map/ppermute | solution.py:313
  130.1 43.1 %collective-permute-start.1 = (bf16[1024,256]{1,0:T(8,128)(2,1)S(1)}, bf16[1024,256]{1,0:T(8,128)(2,1)S(1)}, u32[]{:S(2)}, u32[]{:S(2)}) collective-permute-start(bf16[1024,256]{1,0:T(8,128)(2,1)S(1)} %get-tuple-element.21), channel_id=1, source_target_pairs={{8,0},{12,4},{16,8},{20,12},{24,16},{28,20},{9,1},{13,5},{17,9},{2... | collective-permute-start | bytes 1572872 | tf_op jit(solution)/shard_map/ppermute | solution.py:313
  131.4 44.8 %collective-permute-start.10 = (bf16[1024,256]{1,0:T(8,128)(2,1)S(1)}, bf16[1024,256]{1,0:T(8,128)(2,1)S(1)}, u32[]{:S(2)}, u32[]{:S(2)}) collective-permute-start(bf16[1024,256]{1,0:T(8,128)(2,1)S(1)} %get-tuple-element.16), channel_id=1, source_target_pairs={{0,16},{4,20},{8,24},{12,28},{1,17},{5,21},{9,25},{13,29},{2,18},{... | collective-permute-start | bytes 1572872 | tf_op jit(solution)/shard_map/ppermute | solution.py:313
  138.0 39.0 %collective-permute-start.6 = (bf16[1024,256]{1,0:T(8,128)(2,1)S(1)}, bf16[1024,256]{1,0:T(8,128)(2,1)S(1)}, u32[]{:S(2)}, u32[]{:S(2)}) collective-permute-start(bf16[1024,256]{1,0:T(8,128)(2,1)S(1)} %get-tuple-element.16), channel_id=1, source_target_pairs={{20,24},{16,28},{21,25},{17,29},{22,26},{18,30},{23,27},{19,31}} | collective-permute-start | bytes 1572872 | tf_op jit(solution)/shard_map/ppermute | solution.py:313
  143.5 35.7 %collective-permute-start.9 = (bf16[1024,256]{1,0:T(8,128)(2,1)S(1)}, bf16[1024,256]{1,0:T(8,128)(2,1)S(1)}, u32[]{:S(2)}, u32[]{:S(2)}) collective-permute-start(bf16[1024,256]{1,0:T(8,128)(2,1)S(1)} %get-tuple-element.18), channel_id=1, source_target_pairs={{0,12},{4,16},{8,20},{12,24},{16,28},{1,13},{5,17},{9,21},{13,25},... | collective-permute-start | bytes 1572872 | tf_op jit(solution)/shard_map/ppermute | solution.py:313
  172.6 6.6 %collective-permute-start.4 = (bf16[1024,256]{1,0:T(8,128)(2,1)S(1)}, bf16[1024,256]{1,0:T(8,128)(2,1)S(1)}, u32[]{:S(2)}, u32[]{:S(2)}) collective-permute-start(bf16[1024,256]{1,0:T(8,128)(2,1)S(1)} %get-tuple-element.18), channel_id=1, source_target_pairs={{20,28},{21,29},{22,30},{23,31}} | collective-permute-start | bytes 1572872 | tf_op jit(solution)/shard_map/ppermute | solution.py:313
  173.3 15.9 %collective-permute-start.8 = (bf16[1024,256]{1,0:T(8,128)(2,1)S(1)}, bf16[1024,256]{1,0:T(8,128)(2,1)S(1)}, u32[]{:S(2)}, u32[]{:S(2)}) collective-permute-start(bf16[1024,256]{1,0:T(8,128)(2,1)S(1)} %get-tuple-element.20), channel_id=1, source_target_pairs={{0,8},{4,12},{8,16},{12,20},{16,24},{20,28},{1,9},{5,13},{9,17},{1... | collective-permute-start | bytes 1572872 | tf_op jit(solution)/shard_map/ppermute | solution.py:313
  176.3 12.9 %collective-permute-start.2 = (bf16[1024,256]{1,0:T(8,128)(2,1)S(1)}, bf16[1024,256]{1,0:T(8,128)(2,1)S(1)}, u32[]{:S(2)}, u32[]{:S(2)}) collective-permute-start(bf16[1024,256]{1,0:T(8,128)(2,1)S(1)} %get-tuple-element.20), channel_id=1, source_target_pairs={{24,28},{25,29},{26,30},{27,31}} | collective-permute-start | bytes 1572872 | tf_op jit(solution)/shard_map/ppermute | solution.py:313
  191.2 1.6 copy-start.1
  192.3 1.7 copy-start
Sparse Core Ops, SparseCore 0:
  192.4 38.8 reduce-scatter.1
